TPU v7x, 32 devices: a whole 2x2x4 slice. The times are simulated.
32 devices in a mesh: br: 8 (over z, y), bus: 4 (over x, core).
Axes of the slice: x: 2, y: 2, z: 4, core: 2. Of those that a mesh axis runs over, the one named last changes fastest.
Arguments:
- shift_factors: bfloat16 [65536, 8192], P('br', 'bus'), may hold values from -0.09375 to 0.09375
- injections: float32 [8192, 384], P('bus'), may hold values from -6 to 6
- prices: float32 [65536, 384], P(('br', 'bus')), may hold values from -6 to 6
- limits: float32 [65536], P(('br', 'bus')), may hold values from 0.2 to 2
- unit_cost: float32 [8192], P('bus'), may hold values from -1 to 1
- bus_load: float32 [8192], P('bus'), may hold values from 0.5 to 3
- bus_capacity: float32 [8192], P('bus'), may hold values from 0.5 to 3
- irradiance_profile: float32 [64, 256], replicated, may hold values from 0 to 1
- plant_group: int32 [8192], P('bus'), may hold values from 0 to 255
- scenario_profile: int32 [384], replicated, may hold values from 0 to 63
- listed_slab: int32 [256, 3], replicated, may hold values from 0 to 7, all different within a row; in each aligned block of 8 rows (0 to 7, 8 to 15, ...) at most 6 rows name the same one
- listed_block: int32 [256, 3], replicated, may hold values from 0 to 15
- rent_weight: bfloat16 [256, 1536], P(('br', 'bus')), may hold values from -0.15625 to 0.15625
Outputs:
- new_injections: float32 [8192, 384], P('bus')
- new_prices: float32 [65536, 384], P(('br', 'bus'))
- group_rent: float32 [256, 384], P(('br', 'bus'))
Inputs may be any that keep to these rules, and one draw needn't show every extreme that they name: `listed_slab`: each plant group names 3 different slabs; among the 8 plant groups of one device (aligned blocks of 8 rows) no slab is named by more than 6 groups, and some device's groups name one slab exactly 6 times.
All inputs are finite; a program needn't handle non-finite values.
Results may differ from a plain program's by a relative error of at most 0.0052.
Values may be sent and summed in bfloat16 or wider, within the bound.
A program may use at most 128 MiB of HBM per device.

v0:
```python
import jax
import jax.numpy as jnp
from jax import lax
from jax.sharding import PartitionSpec as P

BLOCK = 512
CAP = 6
GDEV = 8


step_dual = 0.5
step_primal = 0.25


def per_device(
    shift_factors,
    injections,
    prices,
    limits,
    unit_cost,
    bus_load,
    bus_capacity,
    irradiance_profile,
    plant_group,
    scenario_profile,
    listed_slab,
    listed_block,
    rent_weight,
):
    scenarios = injections.shape[1]
    bus_axis = lax.axis_size("bus")
    slab_axis = lax.axis_size("br")
    inject_half = injections.astype(jnp.bfloat16)
    flow = lax.psum_scatter(
        jnp.dot(shift_factors, inject_half, preferred_element_type=jnp.float32),
        "bus",
        scatter_dimension=0,
        tiled=True,
    )
    moved = prices + step_dual * flow
    bound = step_dual * limits[:, None]
    new_prices = moved - jnp.clip(moved, -bound, bound)
    price_half = new_prices.astype(jnp.bfloat16)
    slab_prices = lax.all_gather(price_half, "bus", axis=0, tiled=True)
    partial_grad = lax.dot_general(
        shift_factors, slab_prices, (((0,), (0,)), ((), ())), preferred_element_type=jnp.float32
    )
    gradient = lax.psum(partial_grad, "br")
    group_count = irradiance_profile.shape[1]
    profile_count = irradiance_profile.shape[0]
    pick_group = (plant_group[:, None] == jnp.arange(group_count, dtype=jnp.int32)[None, :]).astype(
        jnp.float32
    )
    bus_profile = jnp.dot(pick_group, irradiance_profile.T, precision=lax.Precision.HIGHEST)
    pick_scenario = (
        jnp.arange(profile_count, dtype=jnp.int32)[:, None] == scenario_profile[None, :]
    ).astype(jnp.float32)
    share = jnp.dot(bus_profile, pick_scenario, precision=lax.Precision.HIGHEST)
    upper = bus_capacity[:, None] * share
    trial = injections - step_primal * (unit_cost[:, None] + gradient)
    new_injections = jnp.minimum(jnp.maximum(trial, -bus_load[:, None]), upper)
    list_len = listed_slab.shape[1]
    entries = GDEV * list_len
    slab_by_device = listed_slab.reshape(-1, entries)
    block_by_device = listed_block.reshape(-1, entries)
    slab_index = lax.axis_index("br")
    column_index = lax.axis_index("bus")
    targets = jnp.arange(slab_axis, dtype=jnp.int32) * bus_axis + column_index
    wanted_slab = jnp.take(slab_by_device, targets, axis=0)
    wanted_block = jnp.take(block_by_device, targets, axis=0)
    matched = wanted_slab == slab_index
    slot_rank = jnp.cumsum(matched.astype(jnp.int32), axis=1) - 1
    slot_range = jnp.arange(CAP, dtype=jnp.int32)
    selected = matched[:, None, :] & (slot_rank[:, None, :] == slot_range[None, :, None])
    block_choice = jnp.sum(jnp.where(selected, wanted_block[:, None, :], 0), axis=2)
    filled = jnp.any(selected, axis=2)
    slab_blocks = slab_prices.reshape(-1, BLOCK, scenarios)
    outgoing = jnp.take(slab_blocks, block_choice, axis=0)
    self_device = slab_index * bus_axis + column_index
    own_slab = lax.dynamic_index_in_dim(slab_by_device, self_device, 0, keepdims=False)
    positions = jnp.arange(entries, dtype=jnp.int32)
    earlier = positions[None, :] < positions[:, None]
    same_slab = own_slab[:, None] == own_slab[None, :]
    own_slot = jnp.sum((same_slab & earlier).astype(jnp.int32), axis=1)
    lookup = own_slab * CAP + own_slot
    outgoing = jnp.where(filled[:, :, None, None], outgoing, jnp.zeros_like(outgoing))
    arrived = lax.all_to_all(outgoing, "br", split_axis=0, concat_axis=0, tiled=True)
    fetched = jnp.take(arrived.reshape(-1, BLOCK, scenarios), lookup, axis=0)
    fetched = fetched.reshape(GDEV, list_len * BLOCK, scenarios)
    group_rent = jnp.einsum("gr,grs->gs", rent_weight, fetched, preferred_element_type=jnp.float32)
    return (new_injections, new_prices, group_rent)


def solution(mesh):
    placed = (
        P("br", "bus"),
        P("bus", None),
        P(("br", "bus"), None),
        P(("br", "bus")),
        P("bus"),
        P("bus"),
        P("bus"),
        P(),
        P("bus"),
        P(),
        P(),
        P(),
        P(("br", "bus"), None),
    )
    return jax.shard_map(
        per_device,
        mesh=mesh,
        in_specs=placed,
        out_specs=(P("bus", None), P(("br", "bus"), None), P(("br", "bus"), None)),
        check_vma=False,
    )
```

profile of v0, /device:TPU:0, one launch (start us, length us, event | category | flops | bytes accessed | tf_op | source)
XLA Modules:
  0.0 770.1 jit_solution(2536803496146330547)
XLA Ops:
  7.2 25.1 %fusion.1 = f32[8192,384]{1,0:T(8,128)} fusion(bf16[8192,2048]{1,0:T(8,128)(2,1)} %param.15, f32[2048,384]{1,0:T(8,128)} %param.16), kind=kOutput, calls=%fused_computation.11 | convolution fusion | flops 12885688320 | bytes 49283072 | tf_op jit(solution)/shard_map/dot_general | solution.py:35
  32.4 0.6 copy-done.5
  33.0 101.2 %reduce-scatter.2.cloned.1.call-done = f32[2048,384]{1,0:T(8,128)} async-done(((f32[8192,384]{1,0:T(8,128)}), f32[2048,384]{1,0:T(8,128)}) %reduce-scatter.2.cloned.1.call-update) | async-done | bytes 3145744 | tf_op jit(solution)/shard_map/reduce_scatter | solution.py:34
  134.2 4.0 fusion.14
  138.8 0.6 gather_fusion.2
  139.3 0.6 gather_fusion.3
  140.0 0.2 reduce_window_sum.11
  140.2 0.2 fusion.8
  141.0 43.8 %all-gather.2.cloned.1.call-done = bf16[8192,384]{1,0:T(8,128)(2,1)} async-done(((bf16[2048,384]{1,0:T(8,128)(2,1)}), bf16[8192,384]{1,0:T(8,128)(2,1)}) %all-gather.2.cloned.1.call-update) | async-done | bytes 6291472 | tf_op jit(solution)/shard_map/all_gather | solution.py:44
  184.8 11.8 %gather_fusion = bf16[48,512,384]{2,1,0:T(8,128)(2,1)} fusion(bf16[16,512,384]{2,1,0:T(8,128)(2,1)} %bitcast.34, s32[1024]{0:T(1024)S(1)} %pad_clamp_fusion.1), kind=kCustom, calls=%fused_computation.2 | custom fusion | bytes 37748928 | tf_op jit(solution)/shard_map/jit(_take)/gather | solution.py:78
  196.5 17.2 %select_select_fusion = bf16[8,6,512,384]{3,2,1,0:T(8,128)(2,1)} fusion(bf16[8,6,512,384]{3,2,1,0:T(8,128)(2,1)} %bitcast.33, pred[8,6]{1,0:T(8,128)(4,1)S(1)} %copy.44, pred[8,6]{1,0:T(8,128)(4,1)S(1)} %copy.42), kind=kLoop, calls=%fused_computation.4 | loop fusion | flops 18874368 | bytes 37748832 | tf_op jit(solution)/shard_map/jit(_where)/select_n | solution.py:86
  213.8 5.9 all-to-all-start
  219.7 0.2 all-reduce.2.cloned.1.call-start
  219.9 22.0 %convolution_bitcast_fusion = f32[2048,384]{0,1:T(8,128)} fusion(bf16[8192,384]{1,0:T(8,128)(2,1)} %all-gather.2.cloned.1.call-done, bf16[8192,2048]{1,0:T(8,128)(2,1)} %param.15), kind=kOutput, calls=%fused_computation.8 | convolution fusion | flops 12884901888 | bytes 42991616 | tf_op jit(solution)/shard_map/dot_general | solution.py:45
  242.0 2.4 copy.37
  244.5 0.2 convert_reduce_fusion
  245.1 2.0 fusion
  247.1 486.4 %all-reduce.2.cloned.1.call-done = f32[2048,384]{0,1:T(8,128)} async-done(((f32[2048,384]{0,1:T(8,128)}), f32[2048,384]{0,1:T(8,128)}) %all-reduce.2.cloned.1.call-update) | async-done | bytes 3145744 | tf_op jit(solution)/shard_map/psum | solution.py:48
  733.5 5.7 multiply_minimum_fusion
  739.2 3.5 copy.46
  742.7 12.8 %gather_fusion.1 = bf16[24,512,384]{2,1,0:T(8,128)(2,1)} fusion(bf16[48,512,384]{2,1,0:T(8,128)(2,1)} %bitcast.6, s32[1024]{0:T(1024)S(1)} %pad_clamp_fusion), kind=kCustom, calls=%fused_computation.3 | custom fusion | bytes 18874464 | tf_op jit(solution)/shard_map/jit(_take)/gather | solution.py:88
  755.5 6.0 bitcast_select_fusion
  761.6 1.3 fusion.4
  762.9 0.6 copy.53
  (55 shorter events, 1.9 us)
Async XLA Ops:
  7.2 237.9 %copy-start = (f32[64,256]{1,0:T(8,128)S(1)}, f32[64,256]{1,0:T(8,128)}, u32[]{:S(2)}) copy-start(f32[64,256]{1,0:T(8,128)} %param.22) | copy-start | bytes 196612
  7.2 127.0 %reduce-scatter.2.cloned.1.call-start = ((), (), s32[]{:S(2)}) async-start(), calls=%async_computation.2 | async-start | bytes 15728640 | tf_op jit(solution)/shard_map/reduce_scatter | solution.py:34
  32.3 0.7 copy-start.5
  32.3 101.9 %copy-start.1 = (f32[2048,384]{1,0:T(8,128)S(1)}, f32[2048,384]{1,0:T(8,128)}, u32[]{:S(2)}) copy-start(f32[2048,384]{1,0:T(8,128)} %param.17) | copy-start | bytes 9437188
  32.3 152.4 %all-gather.2.cloned.1.call-start = ((), (), s32[]{:S(2)}) async-start(), calls=%async_computation.3 | async-start | bytes 7864320 | tf_op jit(solution)/shard_map/all_gather | solution.py:44
  134.2 4.0 copy-start.7
  134.2 4.3 copy-start.8
  213.8 529.0 %all-to-all-start = ((bf16[8,6,512,384]{3,2,1,0:T(8,128)(2,1)}), bf16[8,6,512,384]{3,2,1,0:T(8,128)(2,1)}, u32[]{:S(2)}, u32[]{:S(2)}) async-start(bf16[8,6,512,384]{3,2,1,0:T(8,128)(2,1)} %select_select_fusion), calls=%async_computation.1 | async-start | bytes 37748736 | tf_op jit(solution)/shard_map/all_to_all | solution.py:87
  219.7 513.8 %all-reduce.2.cloned.1.call-start = ((), (), s32[]{:S(2)}) async-start(), calls=%async_computation.4 | async-start | bytes 6291456 | tf_op jit(solution)/shard_map/psum | solution.py:48
  242.0 2.5 copy-start.6
  242.0 3.1 copy-start.10
  242.0 491.5 %copy-start.3 = (f32[2048]{0:T(1024)S(1)}, f32[2048]{0:T(1024)}, u32[]{:S(2)}) copy-start(f32[2048]{0:T(1024)} %param.21) | copy-start | bytes 24580
  242.0 491.5 %copy-start.4 = (f32[2048]{0:T(1024)S(1)}, f32[2048]{0:T(1024)}, u32[]{:S(2)}) copy-start(f32[2048]{0:T(1024)} %param.19) | copy-start | bytes 24580
  242.0 491.5 %copy-start.9 = (s32[384]{0:T(512)S(1)}, s32[384]{0:T(512)}, u32[]{:S(2)}) copy-start(s32[384]{0:T(512)} %param.24) | copy-start | bytes 4612
  755.5 6.0 copy-start.2
Sparse Core Ops, SparseCore 0:
  32.4 101.7 reduce-scatter.1
  138.3 46.3 all-gather.1
  242.1 491.3 all-reduce.1
where the time goes:
time: 770 us
  waiting for transfers between devices  631 us (82%)
  matrix products  56.1 us (7%)
  local copies, waits for them, and re-layouts  34.1 us (4%)
  other arithmetic  28.2 us (4%)
  between operations  14 us (2%)
    psum x1, waiting for transfers between devices, per_device(): gradient = lax.psum(partial_grad, 'br')  486 us
    reduce_scatter x1, waiting for transfers between devices, per_device(): lax.psum_scatter(jnp.dot(shift_factors, inject_half, preferred_element_ty...  101 us
    all_gather x1, waiting for transfers between devices, per_device(): slab_prices = lax.all_gather(price_half, 'bus', axis=0, tiled=True)  43.8 us
    dot_general x1, matrix products, per_device(): jnp.dot(shift_factors, inject_half, preferred_element_type=jnp.float32)  25.1 us
    dot_general x1, matrix products, per_device(): lax.dot_general(shift_factors, slab_prices, (((0,), (0,)), ((), ())), pre...  22 us
    select_n x1, other arithmetic, per_device(): jnp.where(filled[:, :, None, None], outgoing, jnp.zeros_like(outgoing))  17.2 us
  transfers between devices with their start and end apart: 4, of which 3 were waited for; matrix products, arithmetic and copies ran while one was open for 5% of the time, Pallas kernels for 0%

commit v1 on v0

v1 whole, which is shorter than its diff:
```python
import jax
import jax.numpy as jnp
from jax import lax
from jax.sharding import PartitionSpec as P

BLOCK = 512
GDEV = 8


step_dual = 0.5
step_primal = 0.25


def partners(size, bit):
    return [(i, i ^ (1 << bit)) for i in range(size)]


def halving_sum(x, axis, order, wide=()):
    size = x.shape[0]
    levels = size.bit_length() - 1
    me = lax.axis_index(axis)
    rows, width = x.shape[1:]
    x = x.reshape((2,) * levels + (rows, width))
    for bit in order:
        dim = levels - 1 - bit
        mine = (me >> bit) & 1
        keep = lax.dynamic_index_in_dim(x, mine, dim)
        send = lax.dynamic_index_in_dim(x, 1 - mine, dim)
        if bit not in wide:
            send = send.astype(jnp.bfloat16)
        x = keep + lax.ppermute(send, axis, partners(size, bit)).astype(jnp.float32)
    return x.reshape(rows, width)


def doubling_gather(x, axis, order):
    size = lax.axis_size(axis)
    levels = size.bit_length() - 1
    me = lax.axis_index(axis)
    rows, width = x.shape
    x = x.reshape((1,) * levels + (rows, width))
    for bit in reversed(order):
        dim = levels - 1 - bit
        upper = ((me >> bit) & 1) == 1
        other = lax.ppermute(x, axis, partners(size, bit))
        x = jnp.concatenate([jnp.where(upper, other, x), jnp.where(upper, x, other)], axis=dim)
    return x.reshape(size, rows, width)


def per_device(
    shift_factors,
    injections,
    prices,
    limits,
    unit_cost,
    bus_load,
    bus_capacity,
    irradiance_profile,
    plant_group,
    scenario_profile,
    listed_slab,
    listed_block,
    rent_weight,
):
    bus_axis = lax.axis_size("bus")
    slab_axis = lax.axis_size("br")
    slab_index = lax.axis_index("br")
    column_index = lax.axis_index("bus")
    weights = lax.all_gather(rent_weight, "br", axis=0, tiled=True)
    list_len = listed_slab.shape[1]
    groups = weights.shape[0]
    per_slab = shift_factors.shape[0] // BLOCK
    lists = jnp.stack([listed_slab, listed_block], axis=-1)
    lists = lists.reshape(slab_axis, bus_axis, GDEV, list_len, 2)
    lists = lax.dynamic_index_in_dim(lists, column_index, 1, keepdims=False)
    lists = lists.reshape(groups, list_len, 2)
    here = (lists[..., 0] == slab_index)[:, :, None] & (
        lists[..., 1][:, :, None] == jnp.arange(per_slab, dtype=jnp.int32)
    )
    weights = weights.reshape(groups, list_len, BLOCK)
    spread = jnp.zeros((groups, per_slab, BLOCK), weights.dtype)
    for k in range(list_len):
        spread = jnp.where(here[:, k, :, None], weights[:, k, None, :], spread)
    spread = spread.reshape(groups, per_slab * BLOCK)

    inject_half = injections.astype(jnp.bfloat16)
    bound = step_dual * limits[:, None]
    scenarios = injections.shape[1]
    cut = max(128, scenarios // 128 * 2 // 3 * 128)
    bus_order = tuple(range(bus_axis.bit_length() - 1))
    br_order = tuple(range(slab_axis.bit_length() - 1))
    parts = ((0, cut), (cut, scenarios))
    buses = shift_factors.shape[1]
    flows = [
        jnp.dot(shift_factors, inject_half[:, lo:hi], preferred_element_type=jnp.float32)
        for lo, hi in parts
    ]
    new_parts, grad_parts, rent_parts = [], [], []
    for (lo, hi), partial_flow in zip(parts, flows):
        width = hi - lo
        flow = halving_sum(partial_flow.reshape(bus_axis, -1, width), "bus", bus_order, (0,))
        moved = prices[:, lo:hi] + step_dual * flow
        new_part = moved - jnp.clip(moved, -bound, bound)
        new_parts.append(new_part)
        slab_prices = doubling_gather(new_part.astype(jnp.bfloat16), "bus", bus_order)
        slab_prices = slab_prices.reshape(-1, width)
        partial_grad = lax.dot_general(
            shift_factors, slab_prices, (((0,), (0,)), ((), ())), preferred_element_type=jnp.float32
        )
        partial_rent = jnp.dot(spread, slab_prices, preferred_element_type=jnp.float32)
        half = buses // 2
        first = jnp.concatenate(
            [
                partial_grad[:half].reshape(slab_axis, -1, width),
                partial_rent.reshape(slab_axis, GDEV, width),
            ],
            axis=1,
        )
        second = partial_grad[half:].reshape(slab_axis, -1, width)
        first = halving_sum(first, "br", br_order)
        second_order = br_order[1:] + br_order[:1]
        second = halving_sum(second, "br", second_order)
        rent_parts.append(first[half // slab_axis:])
        first = doubling_gather(first[:half // slab_axis].astype(jnp.bfloat16), "br", br_order)
        second = doubling_gather(second.astype(jnp.bfloat16), "br", second_order)
        grad_parts.append(
            jnp.concatenate([first.reshape(half, width), second.reshape(half, width)], axis=0)
        )
    new_prices = jnp.concatenate(new_parts, axis=1)
    gradient = jnp.concatenate(grad_parts, axis=1).astype(jnp.float32)
    group_rent = jnp.concatenate(rent_parts, axis=1)
    group_count = irradiance_profile.shape[1]
    profile_count = irradiance_profile.shape[0]
    pick_group = (plant_group[:, None] == jnp.arange(group_count, dtype=jnp.int32)[None, :]).astype(
        jnp.float32
    )
    bus_profile = jnp.dot(pick_group, irradiance_profile.T, precision=lax.Precision.HIGHEST)
    pick_scenario = (
        jnp.arange(profile_count, dtype=jnp.int32)[:, None] == scenario_profile[None, :]
    ).astype(jnp.float32)
    share = jnp.dot(bus_profile, pick_scenario, precision=lax.Precision.HIGHEST)
    upper = bus_capacity[:, None] * share
    trial = injections - step_primal * (unit_cost[:, None] + gradient)
    new_injections = jnp.minimum(jnp.maximum(trial, -bus_load[:, None]), upper)
    return (new_injections, new_prices, group_rent)


def solution(mesh):
    placed = (
        P("br", "bus"),
        P("bus", None),
        P(("br", "bus"), None),
        P(("br", "bus")),
        P("bus"),
        P("bus"),
        P("bus"),
        P(),
        P("bus"),
        P(),
        P(),
        P(),
        P(("br", "bus"), None),
    )
    return jax.shard_map(
        per_device,
        mesh=mesh,
        in_specs=placed,
        out_specs=(P("bus", None), P(("br", "bus"), None), P(("br", "bus"), None)),
        check_vma=False,
    )
```

time: 770 us -> 260 us (0.34)
  waiting for transfers between devices: 631 us -> 52.6 us
  starting transfers between devices: 6.21 us -> 40.6 us
  blocking collectives: 0 us -> 31.1 us
  matrix products: 56.1 us -> 72.7 us
  between operations: 14 us -> 1.41 us
  local copies, waits for them, and re-layouts: 34.1 us -> 24.4 us
  other arithmetic: 28.2 us -> 36.7 us
    psum x1 -> x0, waiting for transfers between devices: 486 us -> none  [per_device(): gradient = lax.psum(partial_grad, 'br')]
    reduce_scatter x1 -> x0, waiting for transfers between devices: 101 us -> none  [per_device(): lax.psum_scatter(jnp.dot(shift_factors, inject_half, preferred_element_ty...]
    ppermute x0 -> x32, waiting for transfers between devices: none -> 52.6 us  [the longest x16 36.1 us: doubling_gather(): other = lax.ppermute(x, axis, partners(size, bit))]
    all_gather x1 -> x0, waiting for transfers between devices: 43.8 us -> none  [per_device(): slab_prices = lax.all_gather(price_half, 'bus', axis=0, tiled=True)]
    ppermute x0 -> x32, starting transfers between devices: none -> 40.6 us  [the longest x16 23 us: halving_sum(): x = keep + lax.ppermute(send, axis, partners(size, bit)).astype(jnp.float32)]
    all_gather x0 -> x1, blocking collectives: none -> 31.1 us  [per_device(): weights = lax.all_gather(rent_weight, 'br', axis=0, tiled=True)]
    gather x4 -> x0, local copies, waits for them, and re-layouts: 25.6 us -> none  [the longest x1 12.8 us: per_device(): fetched = jnp.take(arrived.reshape(-1, BLOCK, scenarios), lookup, axis=0)]
    select_n x6 -> x17, other arithmetic: 23.4 us -> 7.79 us  [the longest x16 7.2 us: doubling_gather(): jnp.where(upper, other, x)]
  transfers between devices with their start and end apart: 4 -> 32, of which waited for: 3 -> 19; matrix products, arithmetic and copies ran while one was open for 5% -> 32% of each run, Pallas kernels for 0% -> 0%
where the time goes in v1:
time: 260 us
  matrix products  72.7 us (28%)
  waiting for transfers between devices  52.6 us (20%)
  starting transfers between devices  40.6 us (16%)
  other arithmetic  36.7 us (14%)
  blocking collectives  31.1 us (12%)
  local copies, waits for them, and re-layouts  24.4 us (9%)
    ppermute x16, waiting for transfers between devices, doubling_gather(): other = lax.ppermute(x, axis, partners(size, bit))  36.1 us
    dot_general x2, matrix products, per_device(): jnp.dot(shift_factors, inject_half[:, lo:hi], preferred_element_type=jnp....  32.3 us
    all_gather x1, blocking collectives, per_device(): weights = lax.all_gather(rent_weight, 'br', axis=0, tiled=True)  31.1 us
    dot_general x2, matrix products, per_device(): lax.dot_general(shift_factors, slab_prices, (((0,), (0,)), ((), ())), pre...  29.8 us
    ppermute x16, starting transfers between devices, halving_sum(): x = keep + lax.ppermute(send, axis, partners(size, bit)).astype(jnp.float32)  23 us
    ppermute x16, starting transfers between devices, doubling_gather(): other = lax.ppermute(x, axis, partners(size, bit))  17.6 us
    ppermute x16, waiting for transfers between devices, halving_sum(): x = keep + lax.ppermute(send, axis, partners(size, bit)).astype(jnp.float32)  16.5 us
    add x12, other arithmetic, halving_sum(): x = keep + lax.ppermute(send, axis, partners(size, bit)).astype(jnp.float32)  8.18 us
  transfers between devices with their start and end apart: 32, of which 19 were waited for; matrix products, arithmetic and copies ran while one was open for 32% of the time, Pallas kernels for 0%

profile of v1, /device:TPU:0, one launch (start us, length us, event | category | flops | bytes accessed | tf_op | source)
XLA Modules:
  0.0 259.5 jit_solution(1878143523494887268)
XLA Ops:
  2.8 15.2 %fusion.8 = f32[8192,128]{1,0:T(8,128)S(1)} fusion(bf16[8192,2048]{1,0:T(8,128)(2,1)} %param.13, bf16[2048,384]{1,0:T(8,128)(2,1)S(1)} %convert_element_type.110), kind=kOutput, calls=%fused_computation.41 | convolution fusion | flops 4294967296 | bytes 38273024 | tf_op jit(solution)/shard_map/dot_general | solution.py:94
  21.3 17.1 %fusion.1 = f32[8192,256]{1,0:T(8,128)} fusion(bf16[8192,2048]{1,0:T(8,128)(2,1)} %param.13, bf16[2048,384]{1,0:T(8,128)(2,1)S(1)} %copy-done.8), kind=kOutput, calls=%fused_computation.20 | convolution fusion | flops 8589934592 | bytes 42991616 | tf_op jit(solution)/shard_map/dot_general | solution.py:94
  38.4 4.4 %constant_dynamic-slice_fusion.1 = f32[2,1,2048,256]{3,2,1,0:T(8,128)} fusion(f32[2,2,2048,256]{3,2,1,0:T(8,128)} %bitcast.89, s32[]{:T(128)S(6)} %select_n.326), kind=kLoop, calls=%fused_computation.123 | loop fusion | bytes 8388612 | tf_op jit(solution)/shard_map/jit(dynamic_index_in_dim)/dynamic_slice | solution.py:28
  47.1 2.5 collective-permute-start.17
  49.6 31.1 %all_gather.3 = bf16[64,1536]{1,0:T(8,128)(2,1)S(1)} all-gather(bf16[8,1536]{1,0:T(8,128)(2,1)S(1)} %copy-done.9), channel_id=1, replica_groups=mesh['br'=8,'bus'=4] {'br'}, dimensions={0}, use_global_device_ids=true | all-gather | bytes 221184 | tf_op jit(solution)/shard_map/all_gather | solution.py:68
  81.3 2.6 %convert_bitcast_fusion.1 = (bf16[1,1,2048,128]{3,2,1,0:T(8,128)(2,1)}, f32[2048,128]{1,0:T(8,128)}) fusion(f32[2048]{0:T(1024)S(1)} %get-tuple-element.50, f32[2048]{0:T(1024)S(1)} %get-tuple-element.49, bf16[1,1,2048,128]{3,2,1,0:T(8,128)(2,1)S(1)} %collective-permute-done.17, f32[2,1,2048,128]{3,2,1,0:T(8,128)S(1)} %dynamic-slice_add_fusion.1, ...), kind=kLoop, calls=%fused_computation.45 | loop fusion | flops 2097152 | bytes 4210692 | tf_op jit(solution)/shard_map/reshape | solution.py:40
  85.8 7.5 %collective-permute-done.18 = bf16[1,1,2048,128]{3,2,1,0:T(8,128)(2,1)S(1)} collective-permute-done((bf16[1,1,2048,128]{3,2,1,0:T(8,128)(2,1)}, bf16[1,1,2048,128]{3,2,1,0:T(8,128)(2,1)S(1)}, u32[]{:S(2)}, u32[]{:S(2)}) %collective-permute-start.18) | collective-permute-done | bytes 524320 | tf_op jit(solution)/shard_map/ppermute | solution.py:44
  96.7 4.0 %dynamic-slice_add_fusion = f32[2,1,2048,256]{3,2,1,0:T(8,128)S(1)} fusion(f32[2,1,2048,256]{3,2,1,0:T(8,128)} %collective-permute-done, f32[2,2,2048,256]{3,2,1,0:T(8,128)} %bitcast.90, s32[]{:T(128)S(6)} %select_n.325), kind=kLoop, calls=%fused_computation.1 | loop fusion | flops 1048576 | bytes 12582916 | tf_op jit(solution)/shard_map/add | solution.py:31
  103.2 12.9 %convolution_bitcast_fusion.1 = f32[2048,128]{0,1:T(8,128)S(1)} fusion(bf16[8192,128]{1,0:T(8,128)(2,1)S(1)} %bitcast.85, bf16[8192,2048]{1,0:T(8,128)(2,1)} %param.13), kind=kOutput, calls=%fused_computation.5 | convolution fusion | flops 4294967296 | bytes 36700160 | tf_op jit(solution)/shard_map/dot_general | solution.py:106
  123.9 2.6 collective-permute-done.26
  130.3 3.4 %collective-permute-done.27 = bf16[1,1,2,128,128]{3,2,1,0,4:T(2,128)(2,1)S(1)} collective-permute-done((bf16[1,1,2,128,128]{3,2,1,0,4:T(2,128)(2,1)S(1)}, bf16[1,1,2,128,128]{3,2,1,0,4:T(2,128)(2,1)S(1)}, u32[]{:S(2)}, u32[]{:S(2)}) %collective-permute-start.27) | collective-permute-done | bytes 65568 | tf_op jit(solution)/shard_map/ppermute | solution.py:31
  135.6 3.8 %convert_bitcast_fusion = (bf16[1,1,2048,256]{3,2,1,0:T(8,128)(2,1)S(1)}, f32[2048,256]{1,0:T(8,128)}) fusion(f32[2048]{0:T(1024)S(1)} %get-tuple-element.50, f32[2048]{0:T(1024)S(1)} %get-tuple-element.49, bf16[1,1,2048,256]{3,2,1,0:T(8,128)(2,1)} %collective-permute-done.1, f32[2,1,2048,256]{3,2,1,0:T(8,128)} %copy-done.3, s32[]{:T(128)S(6)} %select_n.327, ...), kind=kLoop, calls=%fused_computation.28 | loop fusion | flops 4194304 | bytes 8404996 | tf_op jit(solution)/shard_map/reshape | solution.py:40
  142.2 3.1 %collective-permute-done.22 = bf16[1,1,1,136,128]{4,3,2,1,0:T(8,128)(2,1)S(1)} collective-permute-done((bf16[1,1,1,136,128]{4,3,2,1,0:T(8,128)(2,1)S(1)}, bf16[1,1,1,136,128]{4,3,2,1,0:T(8,128)(2,1)S(1)}, u32[]{:S(2)}, u32[]{:S(2)}) %collective-permute-start.22) | collective-permute-done | bytes 34848 | tf_op jit(solution)/shard_map/ppermute | solution.py:31
  147.2 15.3 %collective-permute-done.2 = bf16[1,1,2048,256]{3,2,1,0:T(8,128)(2,1)S(1)} collective-permute-done((bf16[1,1,2048,256]{3,2,1,0:T(8,128)(2,1)S(1)}, bf16[1,1,2048,256]{3,2,1,0:T(8,128)(2,1)S(1)}, u32[]{:S(2)}, u32[]{:S(2)}) %collective-permute-start.2) | collective-permute-done | bytes 1048608 | tf_op jit(solution)/shard_map/ppermute | solution.py:44
  166.0 3.5 %collective-permute-start.24 = (bf16[2,1,1,128,128]{4,3,2,1,0:T(8,128)(2,1)S(1)}, bf16[2,1,1,128,128]{4,3,2,1,0:T(8,128)(2,1)S(1)}, u32[]{:S(2)}, u32[]{:S(2)}) collective-permute-start(bf16[2,1,1,128,128]{4,3,2,1,0:T(8,128)(2,1)S(1)} %pad_maximum_fusion.15), channel_id=1, source_target_pairs={{0,8},{4,12},{8,0},{12,4},{16,24},{20,28},{24,16},{28,20},{1,9},{5... | collective-permute-start | bytes 196616 | tf_op jit(solution)/shard_map/ppermute | solution.py:44
  170.2 2.6 %collective-permute-start.31 = (bf16[2,1,2,128,128]{3,2,1,0,4:T(2,128)(2,1)S(1)}, bf16[2,1,2,128,128]{3,2,1,0,4:T(2,128)(2,1)S(1)}, u32[]{:S(2)}, u32[]{:S(2)}) collective-permute-start(bf16[2,1,2,128,128]{3,2,1,0,4:T(2,128)(2,1)S(1)} %pad_maximum_fusion.14), channel_id=1, source_target_pairs={{0,8},{4,12},{8,0},{12,4},{16,24},{20,28},{24,16},{28,20},{1,9},{5... | collective-permute-start | bytes 393224 | tf_op jit(solution)/shard_map/ppermute | solution.py:44
  180.4 3.8 %pad_maximum_fusion.1 = f32[2048,384]{1,0:T(8,128)} fusion(f32[2048,128]{1,0:T(8,128)} %get-tuple-element.6, f32[2048,256]{1,0:T(8,128)} %get-tuple-element.4), kind=kLoop, calls=%fused_computation.2 | loop fusion | flops 786432 | bytes 6291456 | tf_op jit(solution)/shard_map/concatenate | solution.py:128
  186.5 16.9 %convolution_bitcast_fusion = f32[2048,256]{0,1:T(8,128)S(1)} fusion(bf16[8192,256]{1,0:T(8,128)(2,1)S(1)} %bitcast.83, bf16[8192,2048]{1,0:T(8,128)(2,1)} %param.13), kind=kOutput, calls=%fused_computation.4 | convolution fusion | flops 8589934592 | bytes 39845888 | tf_op jit(solution)/shard_map/dot_general | solution.py:106
  208.4 3.0 %fusion.21 = f32[2,2,2,8,256]{4,3,2,1,0:T(8,128)S(1)} fusion(bf16[2,2,2,8,8192]{4,3,2,1,0:T(8,128)(2,1)S(1)} %select_n.337, bf16[8192,256,1,1,1]{1,0,4,3,2:T(8,128)(2,1)} %bitcast.84), kind=kOutput, calls=%fused_computation.134 | convolution fusion | flops 268435456 | bytes 5308416 | tf_op jit(solution)/shard_map/dot_general | solution.py:109
  214.6 2.5 collective-permute-start.11
  224.1 3.2 %collective-permute-start.6 = (bf16[1,1,1,136,256]{4,3,2,1,0:T(8,128)(2,1)S(1)}, bf16[1,1,1,136,256]{4,3,2,1,0:T(8,128)(2,1)S(1)}, u32[]{:S(2)}, u32[]{:S(2)}) collective-permute-start(bf16[1,1,1,136,256]{4,3,2,1,0:T(8,128)(2,1)S(1)} %dynamic-slice_convert_fusion.7), channel_id=1, source_target_pairs={{0,16},{4,20},{8,24},{12,28},{16,0},{20,4},{24,8},{28,12},{1,17},{... | collective-permute-start | bytes 208904 | tf_op jit(solution)/shard_map/ppermute | solution.py:31
  238.1 3.6 %collective-permute-done.14 = bf16[1,1,2,128,256]{3,2,1,0,4:T(2,128)(2,1)S(1)} collective-permute-done((bf16[1,1,2,128,256]{3,2,1,0,4:T(2,128)(2,1)S(1)}, bf16[1,1,2,128,256]{3,2,1,0,4:T(2,128)(2,1)S(1)}, u32[]{:S(2)}, u32[]{:S(2)}) %collective-permute-start.14) | collective-permute-done | bytes 131104 | tf_op jit(solution)/shard_map/ppermute | solution.py:44
  246.0 3.0 %collective-permute-done.15 = bf16[2,1,2,128,256]{3,2,1,0,4:T(2,128)(2,1)S(1)} collective-permute-done((bf16[2,1,2,128,256]{3,2,1,0,4:T(2,128)(2,1)S(1)}, bf16[2,1,2,128,256]{3,2,1,0,4:T(2,128)(2,1)S(1)}, u32[]{:S(2)}, u32[]{:S(2)}) %collective-permute-start.15) | collective-permute-done | bytes 262176 | tf_op jit(solution)/shard_map/ppermute | solution.py:44
  254.3 5.2 %multiply_minimum_fusion = f32[2048,384]{1,0:T(8,128)} fusion(f32[2048,384]{1,0:T(8,128)S(1)} %copy-done.6, f32[2048,64]{0,1:T(8,128)} %fusion, bf16[1024,128]{1,0:T(8,128)(2,1)} %bitcast.98, bf16[1024,128]{1,0:T(8,128)(2,1)} %bitcast.99, bf16[1024,256]{1,0:T(8,128)(2,1)} %bitcast.95, bf16[1024,256]{1,0:T(8,128)(2,1)S(1)} %bitcast.96, ...), kind=kOutput, calls=%fused_computation.3 | convolution fusion | flops 615014400 | bytes 8414720 | tf_op jit(solution)/shard_map/dot_general | solution.py:140
  (184 shorter events, 85.1 us)
Async XLA Ops:
  20.1 23.7 %collective-permute-start.16 = (f32[2,1,2048,128]{3,2,1,0:T(8,128)S(1)}, f32[2,1,2048,128]{3,2,1,0:T(8,128)}, u32[]{:S(2)}, u32[]{:S(2)}) collective-permute-start(f32[2,1,2048,128]{3,2,1,0:T(8,128)S(1)} %constant_dynamic-slice_fusion), channel_id=1, source_target_pairs={{0,1},{1,0},{2,3},{3,2},{4,5},{5,4},{6,7},{7,6},{8,9},{9,8},{10,11... | collective-permute-start | bytes 6291464 | tf_op jit(solution)/shard_map/ppermute | solution.py:31
  42.9 53.8 %collective-permute-start = (f32[2,1,2048,256]{3,2,1,0:T(8,128)}, f32[2,1,2048,256]{3,2,1,0:T(8,128)}, u32[]{:S(2)}, u32[]{:S(2)}) collective-permute-start(f32[2,1,2048,256]{3,2,1,0:T(8,128)} %constant_dynamic-slice_fusion.1), channel_id=1, source_target_pairs={{0,1},{1,0},{2,3},{3,2},{4,5},{5,4},{6,7},{7,6},{8,9},{9,8},{10,11... | collective-permute-start | bytes 12582920 | tf_op jit(solution)/shard_map/ppermute | solution.py:31
  47.1 34.2 %collective-permute-start.17 = (bf16[1,1,2048,128]{3,2,1,0:T(8,128)(2,1)}, bf16[1,1,2048,128]{3,2,1,0:T(8,128)(2,1)S(1)}, u32[]{:S(2)}, u32[]{:S(2)}) collective-permute-start(bf16[1,1,2048,128]{3,2,1,0:T(8,128)(2,1)} %dynamic-slice_convert_fusion.1), channel_id=1, source_target_pairs={{0,2},{1,3},{2,0},{3,1},{4,6},{5,7},{6,4},{7,5},{8,10},{9,11},{10,... | collective-permute-start | bytes 1572872 | tf_op jit(solution)/shard_map/ppermute | solution.py:31
  83.9 9.4 %collective-permute-start.18 = (bf16[1,1,2048,128]{3,2,1,0:T(8,128)(2,1)}, bf16[1,1,2048,128]{3,2,1,0:T(8,128)(2,1)S(1)}, u32[]{:S(2)}, u32[]{:S(2)}) collective-permute-start(bf16[1,1,2048,128]{3,2,1,0:T(8,128)(2,1)} %get-tuple-element.5), channel_id=1, source_target_pairs={{0,2},{1,3},{2,0},{3,1},{4,6},{5,7},{6,4},{7,5},{8,10},{9,11},{10,... | collective-permute-start | bytes 1572872 | tf_op jit(solution)/shard_map/ppermute | solution.py:44
  94.6 8.0 %collective-permute-start.19 = (bf16[2,1,2048,128]{3,2,1,0:T(8,128)(2,1)S(1)}, bf16[2,1,2048,128]{3,2,1,0:T(8,128)(2,1)S(1)}, u32[]{:S(2)}, u32[]{:S(2)}) collective-permute-start(bf16[2,1,2048,128]{3,2,1,0:T(8,128)(2,1)S(1)} %pad_maximum_fusion.4), channel_id=1, source_target_pairs={{0,1},{1,0},{2,3},{3,2},{4,5},{5,4},{6,7},{7,6},{8,9},{9,8},{10,11... | collective-permute-start | bytes 3145736 | tf_op jit(solution)/shard_map/ppermute | solution.py:44
  101.9 33.7 %collective-permute-start.1 = (bf16[1,1,2048,256]{3,2,1,0:T(8,128)(2,1)}, bf16[1,1,2048,256]{3,2,1,0:T(8,128)(2,1)}, u32[]{:S(2)}, u32[]{:S(2)}) collective-permute-start(bf16[1,1,2048,256]{3,2,1,0:T(8,128)(2,1)} %dynamic-slice_convert_fusion), channel_id=1, source_target_pairs={{0,2},{1,3},{2,0},{3,1},{4,6},{5,7},{6,4},{7,5},{8,10},{9,11},{10,... | collective-permute-start | bytes 3145736 | tf_op jit(solution)/shard_map/ppermute | solution.py:31
  122.4 6.6 %collective-permute-start.20 = (bf16[2,2,1,136,128]{4,3,2,1,0:T(8,128)(2,1)S(1)}, bf16[2,2,1,136,128]{4,3,2,1,0:T(8,128)(2,1)S(1)}, u32[]{:S(2)}, u32[]{:S(2)}) collective-permute-start(bf16[2,2,1,136,128]{4,3,2,1,0:T(8,128)(2,1)S(1)} %fusion.11), channel_id=1, source_target_pairs={{0,4},{4,0},{8,12},{12,8},{16,20},{20,16},{24,28},{28,24},{1,5},{5... | collective-permute-start | bytes 417800 | tf_op jit(solution)/shard_map/ppermute | solution.py:31
  127.6 6.1 %collective-permute-start.27 = (bf16[1,1,2,128,128]{3,2,1,0,4:T(2,128)(2,1)S(1)}, bf16[1,1,2,128,128]{3,2,1,0,4:T(2,128)(2,1)S(1)}, u32[]{:S(2)}, u32[]{:S(2)}) collective-permute-start(bf16[1,1,2,128,128]{3,2,1,0,4:T(2,128)(2,1)S(1)} %dynamic-slice_convert_fusion.8), channel_id=1, source_target_pairs={{0,16},{4,20},{8,24},{12,28},{16,0},{20,4},{24,8},{28,12},{1,17},{... | collective-permute-start | bytes 196616 | tf_op jit(solution)/shard_map/ppermute | solution.py:31
  129.0 10.9 %collective-permute-start.21 = (bf16[2,1,1,136,128]{4,3,2,1,0:T(8,128)(2,1)S(1)}, bf16[2,1,1,136,128]{4,3,2,1,0:T(8,128)(2,1)S(1)}, u32[]{:S(2)}, u32[]{:S(2)}) collective-permute-start(bf16[2,1,1,136,128]{4,3,2,1,0:T(8,128)(2,1)S(1)} %dynamic-slice_convert_fusion.6), channel_id=1, source_target_pairs={{0,8},{4,12},{8,0},{12,4},{16,24},{20,28},{24,16},{28,20},{1,9},{5... | collective-permute-start | bytes 208904 | tf_op jit(solution)/shard_map/ppermute | solution.py:31
  133.9 8.1 %collective-permute-start.28 = (bf16[1,1,1,128,128]{3,2,1,0,4:T(2,128)(2,1)S(1)}, bf16[1,1,1,128,128]{3,2,1,0,4:T(2,128)(2,1)S(1)}, u32[]{:S(2)}, u32[]{:S(2)}) collective-permute-start(bf16[1,1,1,128,128]{3,2,1,0,4:T(2,128)(2,1)S(1)} %dynamic-slice_convert_fusion.11), channel_id=1, source_target_pairs={{0,4},{4,0},{8,12},{12,8},{16,20},{20,16},{24,28},{28,24},{1,5},{5... | collective-permute-start | bytes 98312 | tf_op jit(solution)/shard_map/ppermute | solution.py:31
  139.4 23.1 %collective-permute-start.2 = (bf16[1,1,2048,256]{3,2,1,0:T(8,128)(2,1)S(1)}, bf16[1,1,2048,256]{3,2,1,0:T(8,128)(2,1)S(1)}, u32[]{:S(2)}, u32[]{:S(2)}) collective-permute-start(bf16[1,1,2048,256]{3,2,1,0:T(8,128)(2,1)S(1)} %get-tuple-element.3), channel_id=1, source_target_pairs={{0,2},{1,3},{2,0},{3,1},{4,6},{5,7},{6,4},{7,5},{8,10},{9,11},{10,... | collective-permute-start | bytes 3145736 | tf_op jit(solution)/shard_map/ppermute | solution.py:44
  145.4 20.6 %collective-permute-start.23 = (bf16[1,1,1,128,128]{4,3,2,1,0:T(8,128)(2,1)S(1)}, bf16[1,1,1,128,128]{4,3,2,1,0:T(8,128)(2,1)S(1)}, u32[]{:S(2)}, u32[]{:S(2)}) collective-permute-start(bf16[1,1,1,128,128]{4,3,2,1,0:T(8,128)(2,1)S(1)} %slice.125), channel_id=1, source_target_pairs={{0,16},{4,20},{8,24},{12,28},{16,0},{20,4},{24,8},{28,12},{1,17},{... | collective-permute-start | bytes 98312 | tf_op jit(solution)/shard_map/ppermute | solution.py:44
  164.1 20.1 %collective-permute-start.3 = (bf16[2,1,2048,256]{3,2,1,0:T(8,128)(2,1)}, bf16[2,1,2048,256]{3,2,1,0:T(8,128)(2,1)}, u32[]{:S(2)}, u32[]{:S(2)}) collective-permute-start(bf16[2,1,2048,256]{3,2,1,0:T(8,128)(2,1)} %pad_maximum_fusion.2), channel_id=1, source_target_pairs={{0,1},{1,0},{2,3},{3,2},{4,5},{5,4},{6,7},{7,6},{8,9},{9,8},{10,11... | collective-permute-start | bytes 6291464 | tf_op jit(solution)/shard_map/ppermute | solution.py:44
  166.0 6.8 %collective-permute-start.24 = (bf16[2,1,1,128,128]{4,3,2,1,0:T(8,128)(2,1)S(1)}, bf16[2,1,1,128,128]{4,3,2,1,0:T(8,128)(2,1)S(1)}, u32[]{:S(2)}, u32[]{:S(2)}) collective-permute-start(bf16[2,1,1,128,128]{4,3,2,1,0:T(8,128)(2,1)S(1)} %pad_maximum_fusion.15), channel_id=1, source_target_pairs={{0,8},{4,12},{8,0},{12,4},{16,24},{20,28},{24,16},{28,20},{1,9},{5... | collective-permute-start | bytes 196616 | tf_op jit(solution)/shard_map/ppermute | solution.py:44
  170.2 6.0 %collective-permute-start.31 = (bf16[2,1,2,128,128]{3,2,1,0,4:T(2,128)(2,1)S(1)}, bf16[2,1,2,128,128]{3,2,1,0,4:T(2,128)(2,1)S(1)}, u32[]{:S(2)}, u32[]{:S(2)}) collective-permute-start(bf16[2,1,2,128,128]{3,2,1,0,4:T(2,128)(2,1)S(1)} %pad_maximum_fusion.14), channel_id=1, source_target_pairs={{0,8},{4,12},{8,0},{12,4},{16,24},{20,28},{24,16},{28,20},{1,9},{5... | collective-permute-start | bytes 393224 | tf_op jit(solution)/shard_map/ppermute | solution.py:44
  207.4 6.7 %collective-permute-start.10 = (bf16[2,1,2,128,256]{3,2,1,0,4:T(2,128)(2,1)}, bf16[2,1,2,128,256]{3,2,1,0,4:T(2,128)(2,1)S(1)}, u32[]{:S(2)}, u32[]{:S(2)}) collective-permute-start(bf16[2,1,2,128,256]{3,2,1,0,4:T(2,128)(2,1)} %dynamic-slice_convert_fusion.2), channel_id=1, source_target_pairs={{0,8},{4,12},{8,0},{12,4},{16,24},{20,28},{24,16},{28,20},{1,9},{5... | collective-permute-start | bytes 786440 | tf_op jit(solution)/shard_map/ppermute | solution.py:31
  211.8 7.0 %collective-permute-start.4 = (bf16[2,2,1,136,256]{4,3,2,1,0:T(8,128)(2,1)S(1)}, bf16[2,2,1,136,256]{4,3,2,1,0:T(8,128)(2,1)S(1)}, u32[]{:S(2)}, u32[]{:S(2)}) collective-permute-start(bf16[2,2,1,136,256]{4,3,2,1,0:T(8,128)(2,1)S(1)} %fusion.5), channel_id=1, source_target_pairs={{0,4},{4,0},{8,12},{12,8},{16,20},{20,16},{24,28},{28,24},{1,5},{5... | collective-permute-start | bytes 835592 | tf_op jit(solution)/shard_map/ppermute | solution.py:31
  214.6 7.4 %collective-permute-start.11 = (bf16[1,1,2,128,256]{3,2,1,0,4:T(2,128)(2,1)S(1)}, bf16[1,1,2,128,256]{3,2,1,0,4:T(2,128)(2,1)S(1)}, u32[]{:S(2)}, u32[]{:S(2)}) collective-permute-start(bf16[1,1,2,128,256]{3,2,1,0,4:T(2,128)(2,1)S(1)} %dynamic-slice_convert_fusion.5), channel_id=1, source_target_pairs={{0,16},{4,20},{8,24},{12,28},{16,0},{20,4},{24,8},{28,12},{1,17},{... | collective-permute-start | bytes 393224 | tf_op jit(solution)/shard_map/ppermute | solution.py:31
  222.2 6.3 %collective-permute-start.12 = (bf16[1,1,1,128,256]{3,2,1,0,4:T(2,128)(2,1)S(1)}, bf16[1,1,1,128,256]{3,2,1,0,4:T(2,128)(2,1)S(1)}, u32[]{:S(2)}, u32[]{:S(2)}) collective-permute-start(bf16[1,1,1,128,256]{3,2,1,0,4:T(2,128)(2,1)S(1)} %dynamic-slice_convert_fusion.9), channel_id=1, source_target_pairs={{0,4},{4,0},{8,12},{12,8},{16,20},{20,16},{24,28},{28,24},{1,5},{5... | collective-permute-start | bytes 196616 | tf_op jit(solution)/shard_map/ppermute | solution.py:31
  224.1 7.5 %collective-permute-start.6 = (bf16[1,1,1,136,256]{4,3,2,1,0:T(8,128)(2,1)S(1)}, bf16[1,1,1,136,256]{4,3,2,1,0:T(8,128)(2,1)S(1)}, u32[]{:S(2)}, u32[]{:S(2)}) collective-permute-start(bf16[1,1,1,136,256]{4,3,2,1,0:T(8,128)(2,1)S(1)} %dynamic-slice_convert_fusion.7), channel_id=1, source_target_pairs={{0,16},{4,20},{8,24},{12,28},{16,0},{20,4},{24,8},{28,12},{1,17},{... | collective-permute-start | bytes 208904 | tf_op jit(solution)/shard_map/ppermute | solution.py:31
  234.4 7.4 %collective-permute-start.14 = (bf16[1,1,2,128,256]{3,2,1,0,4:T(2,128)(2,1)S(1)}, bf16[1,1,2,128,256]{3,2,1,0,4:T(2,128)(2,1)S(1)}, u32[]{:S(2)}, u32[]{:S(2)}) collective-permute-start(bf16[1,1,2,128,256]{3,2,1,0,4:T(2,128)(2,1)S(1)} %pad_maximum_fusion.12), channel_id=1, source_target_pairs={{0,16},{4,20},{8,24},{12,28},{16,0},{20,4},{24,8},{28,12},{1,17},{... | collective-permute-start | bytes 393224 | tf_op jit(solution)/shard_map/ppermute | solution.py:44
  237.1 7.3 %collective-permute-start.8 = (bf16[2,1,1,128,256]{4,3,2,1,0:T(8,128)(2,1)S(1)}, bf16[2,1,1,128,256]{4,3,2,1,0:T(8,128)(2,1)S(1)}, u32[]{:S(2)}, u32[]{:S(2)}) collective-permute-start(bf16[2,1,1,128,256]{4,3,2,1,0:T(8,128)(2,1)S(1)} %pad_maximum_fusion.11), channel_id=1, source_target_pairs={{0,8},{4,12},{8,0},{12,4},{16,24},{20,28},{24,16},{28,20},{1,9},{5... | collective-permute-start | bytes 393224 | tf_op jit(solution)/shard_map/ppermute | solution.py:44
  242.6 6.4 %collective-permute-start.15 = (bf16[2,1,2,128,256]{3,2,1,0,4:T(2,128)(2,1)S(1)}, bf16[2,1,2,128,256]{3,2,1,0,4:T(2,128)(2,1)S(1)}, u32[]{:S(2)}, u32[]{:S(2)}) collective-permute-start(bf16[2,1,2,128,256]{3,2,1,0,4:T(2,128)(2,1)S(1)} %pad_maximum_fusion.8), channel_id=1, source_target_pairs={{0,8},{4,12},{8,0},{12,4},{16,24},{20,28},{24,16},{28,20},{1,9},{5... | collective-permute-start | bytes 786440 | tf_op jit(solution)/shard_map/ppermute | solution.py:44
  245.2 8.0 %collective-permute-start.9 = (bf16[2,2,1,128,256]{4,3,2,1,0:T(8,128)(2,1)}, bf16[2,2,1,128,256]{4,3,2,1,0:T(8,128)(2,1)}, u32[]{:S(2)}, u32[]{:S(2)}) collective-permute-start(bf16[2,2,1,128,256]{4,3,2,1,0:T(8,128)(2,1)} %pad_maximum_fusion.7), channel_id=1, source_target_pairs={{0,4},{4,0},{8,12},{12,8},{16,20},{20,16},{24,28},{28,24},{1,5},{5... | collective-permute-start | bytes 786440 | tf_op jit(solution)/shard_map/ppermute | solution.py:44
  (26 other events, 264.2 us)
